TPU v7x, 32 devices: a whole 2x2x4 slice. The times are simulated.
32 devices in a mesh: seq: 16 (over z, y, x), wa: 2 (over core).
Axes of the slice: x: 2, y: 2, z: 4, core: 2. Of those that a mesh axis runs over, the one named last changes fastest.
Arguments:
- tokens: bfloat16 [16384, 1024], P(('seq', 'wa')), may hold values from -6 to 6
- cotangent: bfloat16 [16384, 1024], P(('seq', 'wa')), may hold values from -6 to 6
- doc_lengths: int32 [32], replicated, may hold values from 1 to 4096, as said below
- norm_gain: bfloat16 [1024], P('wa'), may hold values from 0.25 to 1.75
- in_weight: bfloat16 [1024, 3072], P('wa'), may hold values from -0.1875 to 0.1875
- conv_taps: bfloat16 [1024, 3], P('wa'), may hold values from -3.5 to 3.5
- out_weight: bfloat16 [1024, 1024], P('wa'), may hold values from -0.1875 to 0.1875
- ffn_gain: bfloat16 [1024], P('wa'), may hold values from 0.25 to 1.75
- gate_weight: bfloat16 [1024, 4608], P('wa'), may hold values from -0.1875 to 0.1875
- up_weight: bfloat16 [1024, 4608], P('wa'), may hold values from -0.1875 to 0.1875
- down_weight: bfloat16 [4608, 1024], P('wa'), may hold values from -0.09375 to 0.09375
Outputs:
- block_out: bfloat16 [16384, 1024], P(('seq', 'wa'))
- input_grad: bfloat16 [16384, 1024], P(('seq', 'wa'))
- norm_gain_grad: float32 [1024], P(('seq', 'wa'))
- in_weight_grad: float32 [1024, 3072], P(('seq', 'wa'))
- conv_taps_grad: float32 [1024, 3], P(('seq', 'wa'))
- out_weight_grad: float32 [1024, 1024], P(('seq', 'wa'))
- ffn_gain_grad: float32 [1024], P(('seq', 'wa'))
- gate_weight_grad: float32 [1024, 4608], P(('seq', 'wa'))
- up_weight_grad: float32 [1024, 4608], P(('seq', 'wa'))
- down_weight_grad: float32 [4608, 1024], P(('seq', 'wa'))
Inputs may be any that keep to these rules, and one draw needn't show every extreme that they name: `doc_lengths`: lengths of the 32 documents laid end to end in stream order, summing to 16384; the first document has exactly 4096 tokens.
All inputs are finite; a program needn't handle non-finite values.
Results may differ from a plain program's by a relative error of at most 0.0086.
Values may be sent and summed in bfloat16 or wider, within the bound.
No kernel may reach another device: no remote copies, remote signals or barrier semaphores. Data moves between devices by JAX's collectives and lax.ppermute only.
A program may use at most 256 MiB of HBM per device.

v0:
```python
import jax
import jax.numpy as jnp
from jax import lax
from jax.sharding import PartitionSpec as P

epsilon = 1e-05


def shifted(value, axis, steps):
    count = lax.axis_size(axis)
    first, last = (max(0, -steps), min(count, count - steps))
    return lax.ppermute(value, axis, [(source, source + steps) for source in range(first, last)])


def left_dot(left, right):
    return lax.dot_general(
        left, right, (((0,), (0,)), ((), ())), preferred_element_type=jnp.float32
    )


def right_dot(left, right):
    return lax.dot_general(
        left, right, (((1,), (1,)), ((), ())), preferred_element_type=jnp.float32
    )


def plain_dot(left, right):
    return jnp.dot(left, right, preferred_element_type=jnp.float32)


def norm_back(grad_norm, normed, scale, gain):
    inner = grad_norm * gain
    return scale * (inner - normed * jnp.mean(inner * normed, axis=-1, keepdims=True))


def local(
    tokens,
    cotangent,
    doc_lengths,
    norm_gain,
    in_weight,
    conv_taps,
    out_weight,
    ffn_gain,
    gate_weight,
    up_weight,
    down_weight,
):
    rows, width = tokens.shape
    place = lax.axis_index(("seq", "wa")) * rows + jnp.arange(rows, dtype=jnp.int32)
    starts = jnp.cumsum(doc_lengths) - doc_lengths
    first = jnp.any(place[:, None] == starts[None, :], axis=1)
    before = jnp.any((place - 1)[:, None] == starts[None, :], axis=1)
    keep_one = jnp.where(first, 0.0, 1.0).astype(jnp.float32)[:, None]
    keep_two = jnp.where(jnp.logical_or(first, before), 0.0, 1.0).astype(jnp.float32)[:, None]
    shards = (
        norm_gain,
        ffn_gain,
        conv_taps,
        in_weight,
        out_weight,
        gate_weight,
        up_weight,
        down_weight,
    )
    gathered = (
        lax.all_gather(shards[0], "wa", axis=0, tiled=True),
        lax.all_gather(shards[1], "wa", axis=0, tiled=True),
        lax.all_gather(shards[2], "wa", axis=0, tiled=True),
        lax.all_gather(shards[3], "wa", axis=0, tiled=True),
        lax.all_gather(shards[4], "wa", axis=0, tiled=True),
        lax.all_gather(shards[5], "wa", axis=0, tiled=True),
        lax.all_gather(shards[6], "wa", axis=0, tiled=True),
        lax.all_gather(shards[7], "wa", axis=0, tiled=True),
    )
    gain_one = gathered[0].astype(jnp.float32)
    gain_two = gathered[1].astype(jnp.float32)
    taps = gathered[2].astype(jnp.float32)
    w_in, w_out, w_gate, w_up, w_down = gathered[3:]
    resid = tokens.astype(jnp.float32)
    scale_one = lax.rsqrt(jnp.mean(resid * resid, axis=-1, keepdims=True) + epsilon)
    normed_one = resid * scale_one
    norm_in = (normed_one * gain_one).astype(jnp.bfloat16)
    proj = plain_dot(norm_in, w_in)
    b_part = proj[:, :width]
    c_part = proj[:, width : 2 * width]
    x_part = proj[:, 2 * width :]
    mixed_in = b_part * x_part
    previous = shifted(mixed_in[-2:], ("seq", "wa"), 1)
    extended = jnp.concatenate([previous, mixed_in], axis=0)
    back_one = extended[1:-1]
    back_two = extended[:-2]
    conv = (
        taps[:, 0] * mixed_in + keep_one * taps[:, 1] * back_one + keep_two * taps[:, 2] * back_two
    )
    gated = (c_part * conv).astype(jnp.bfloat16)
    hidden_res = resid + plain_dot(gated, w_out)
    scale_two = lax.rsqrt(jnp.mean(hidden_res * hidden_res, axis=-1, keepdims=True) + epsilon)
    normed_two = hidden_res * scale_two
    norm_ffn = (normed_two * gain_two).astype(jnp.bfloat16)
    gate = plain_dot(norm_ffn, w_gate)
    up_val = plain_dot(norm_ffn, w_up)
    sigma = jax.nn.sigmoid(gate)
    silu_gate = gate * sigma
    act = (silu_gate * up_val).astype(jnp.bfloat16)
    block_out = (hidden_res + plain_dot(act, w_down)).astype(jnp.bfloat16)
    down_grad = left_dot(act, cotangent)
    d_act = right_dot(cotangent, w_down)
    d_up = (d_act * silu_gate).astype(jnp.bfloat16)
    d_gate = (d_act * up_val * sigma * (1.0 + gate * (1.0 - sigma))).astype(jnp.bfloat16)
    gate_grad = left_dot(norm_ffn, d_gate)
    up_grad = left_dot(norm_ffn, d_up)
    d_norm_ffn = right_dot(d_gate, w_gate) + right_dot(d_up, w_up)
    gain_two_grad = jnp.sum(d_norm_ffn * normed_two, axis=0)
    d_hidden = cotangent.astype(jnp.float32) + norm_back(
        d_norm_ffn, normed_two, scale_two, gain_two
    )
    d_branch = d_hidden.astype(jnp.bfloat16)
    out_grad = left_dot(gated, d_branch)
    d_gated = right_dot(d_branch, w_out)
    d_c = d_gated * conv
    d_conv = d_gated * c_part
    tap_terms = jnp.stack(
        [
            jnp.sum(d_conv * mixed_in, axis=0),
            jnp.sum(keep_one * d_conv * back_one, axis=0),
            jnp.sum(keep_two * d_conv * back_two, axis=0),
        ],
        axis=0,
    )
    taps_grad = tap_terms.T
    along_one = keep_one * d_conv * taps[:, 1]
    along_two = keep_two * d_conv * taps[:, 2]
    zero_row = jnp.zeros((1, width), jnp.float32)
    d_mixed = (
        taps[:, 0] * d_conv
        + jnp.concatenate([along_one[1:], zero_row], axis=0)
        + jnp.concatenate([along_two[2:], zero_row, zero_row], axis=0)
    )
    head_grad = jnp.concatenate([along_two[0:1], along_one[0:1] + along_two[1:2]], axis=0)
    returned = shifted(head_grad, ("seq", "wa"), -1)
    d_mixed = jnp.concatenate([d_mixed[:-2], d_mixed[-2:] + returned], axis=0)
    d_proj = jnp.concatenate([d_mixed * x_part, d_c, d_mixed * b_part], axis=1).astype(jnp.bfloat16)
    in_grad = left_dot(norm_in, d_proj)
    d_norm_in = right_dot(d_proj, w_in)
    gain_one_grad = jnp.sum(d_norm_in * normed_one, axis=0)
    input_grad = (d_hidden + norm_back(d_norm_in, normed_one, scale_one, gain_one)).astype(
        jnp.bfloat16
    )
    partials = (
        gain_one_grad,
        in_grad,
        taps_grad,
        out_grad,
        gain_two_grad,
        gate_grad,
        up_grad,
        down_grad,
    )
    summed = (
        lax.psum_scatter(partials[0], ("seq", "wa"), scatter_dimension=0, tiled=True),
        lax.psum_scatter(partials[1], ("seq", "wa"), scatter_dimension=0, tiled=True),
        lax.psum_scatter(partials[2], ("seq", "wa"), scatter_dimension=0, tiled=True),
        lax.psum_scatter(partials[3], ("seq", "wa"), scatter_dimension=0, tiled=True),
        lax.psum_scatter(partials[4], ("seq", "wa"), scatter_dimension=0, tiled=True),
        lax.psum_scatter(partials[5], ("seq", "wa"), scatter_dimension=0, tiled=True),
        lax.psum_scatter(partials[6], ("seq", "wa"), scatter_dimension=0, tiled=True),
        lax.psum_scatter(partials[7], ("seq", "wa"), scatter_dimension=0, tiled=True),
    )
    return (block_out, input_grad) + tuple(summed)


def solution(mesh):
    placed = (
        P(("seq", "wa"), None),
        P(("seq", "wa"), None),
        P(),
        P("wa"),
        P("wa", None),
        P("wa", None),
        P("wa", None),
        P("wa"),
        P("wa", None),
        P("wa", None),
        P("wa", None),
    )
    return jax.shard_map(
        local,
        mesh=mesh,
        in_specs=placed,
        out_specs=(
            P(("seq", "wa"), None),
            P(("seq", "wa"), None),
            P(("seq", "wa")),
            P(("seq", "wa"), None),
            P(("seq", "wa"), None),
            P(("seq", "wa"), None),
            P(("seq", "wa")),
            P(("seq", "wa"), None),
            P(("seq", "wa"), None),
            P(("seq", "wa"), None),
        ),
        check_vma=False,
    )
```

profile of v0, /device:TPU:0, one launch (start us, length us, event | category | flops | bytes accessed | tf_op | source)
XLA Modules:
  0.0 1239.9 jit_solution(15673625876714211404)
XLA Ops:
  10.9 1.9 all-gather
  12.9 1.8 all_gather.26
  15.1 13.9 %all-gather.8.cloned.1.call-done = bf16[1024,3072]{1,0:T(8,128)(2,1)} async-done(((bf16[512,3072]{1,0:T(8,128)(2,1)}), bf16[1024,3072]{1,0:T(8,128)(2,1)}) %all-gather.8.cloned.1.call-update) | async-done | bytes 6291472 | tf_op jit(solution)/shard_map/all_gather | solution.py:70
  29.0 5.7 fusion.21
  35.4 2.1 collective-permute-start
  37.6 3.3 all-gather.1
  40.9 2.4 multiply_convert_fusion.7
  43.3 3.3 multiply_reduce_fusion.5
  48.1 18.9 %all-gather.12.cloned.1.call-done = bf16[1024,4608]{1,0:T(8,128)(2,1)} async-done(((bf16[512,4608]{1,0:T(8,128)(2,1)}), bf16[1024,4608]{1,0:T(8,128)(2,1)}) %all-gather.12.cloned.1.call-update) | async-done | bytes 9437200 | tf_op jit(solution)/shard_map/all_gather | solution.py:72
  67.0 11.4 fusion.27
  78.4 13.0 %all-gather.14.cloned.1.call-done = bf16[1024,4608]{1,0:T(8,128)(2,1)} async-done(((bf16[512,4608]{1,0:T(8,128)(2,1)}), bf16[1024,4608]{1,0:T(8,128)(2,1)}) %all-gather.14.cloned.1.call-update) | async-done | bytes 9437200 | tf_op jit(solution)/shard_map/all_gather | solution.py:73
  91.4 11.4 fusion.28
  102.9 13.0 %all-gather.16.cloned.1.call-done = bf16[4608,1024]{1,0:T(8,128)(2,1)} async-done(((bf16[2304,1024]{1,0:T(8,128)(2,1)}), bf16[4608,1024]{1,0:T(8,128)(2,1)}) %all-gather.16.cloned.1.call-update) | async-done | bytes 9437200 | tf_op jit(solution)/shard_map/all_gather | solution.py:74
  115.9 18.0 %multiply_convert_fusion = (bf16[512,4608]{1,0:T(8,128)(2,1)}, bf16[512,4608]{1,0:T(8,128)(2,1)}, bf16[512,4608]{1,0:T(8,128)(2,1)}) fusion(f32[512,4608]{1,0:T(8,128)} %fusion.27, f32[512,4608]{1,0:T(8,128)} %fusion.28, bf16[512,1024]{1,0:T(8,128)(2,1)} %param.12, bf16[4608,1024]{1,0:T(8,128)(2,1)} %all-gather.16.cloned.1.call-done), kind=kOutput, calls=%fused_computation | convolution fusion | flops 4867227648 | bytes 43515904 | tf_op jit(solution)/shard_map/dot_general | solution.py:22
  133.9 9.2 fusion.29
  143.1 8.3 multiply_reduce_fusion
  155.4 3.8 multiply_reduce_fusion.2
  160.6 4.9 fusion.16
  173.7 6.8 fusion.14
  180.6 11.8 fusion.30
  192.5 11.5 fusion.31
  205.2 11.5 fusion.32
  218.3 9.9 add_convert_fusion
  228.3 7.9 fusion.12
  236.2 42.6 %all-reduce.4 = (f32[1024]{0:T(1024)S(1)}, f32[1024]{0:T(1024)S(1)}) all-reduce(f32[1024]{0:T(1024)S(1)} %get-tuple-element.15, f32[1024]{0:T(1024)S(1)} %get-tuple-element.12), channel_id=2, replica_groups=mesh['seq'=16,'wa'=2] {'seq','wa'}, use_global_device_ids=true, to_apply=%region_8.9.clone | all-reduce | flops 2048 | bytes 16384
  279.9 3.1 fusion.11
  283.1 12.8 %reduce-scatter.19.cloned.1.call-done = f32[32,3]{1,0:T(8,128)} async-done(((f32[1024,3]{1,0:T(8,128)}), f32[32,3]{1,0:T(8,128)}) %reduce-scatter.19.cloned.1.call-update) | async-done | bytes 400
  297.2 138.8 %reduce-scatter.11.cloned.1.call-done = f32[32,1024]{1,0:T(8,128)} async-done(((f32[1024,1024]{1,0:T(8,128)}), f32[32,1024]{1,0:T(8,128)}) %reduce-scatter.11.cloned.1.call-update) | async-done | bytes 131088 | tf_op jit(solution)/shard_map/reduce_scatter | solution.py:164
  436.0 158.9 %reduce-scatter.9.cloned.1.call-done = f32[32,3072]{1,0:T(8,128)} async-done(((f32[1024,3072]{1,0:T(8,128)}), f32[32,3072]{1,0:T(8,128)}) %reduce-scatter.9.cloned.1.call-update) | async-done | bytes 393232 | tf_op jit(solution)/shard_map/reduce_scatter | solution.py:162
  594.9 212.9 %reduce-scatter.13.cloned.1.call-done = f32[32,4608]{1,0:T(8,128)} async-done(((f32[1024,4608]{1,0:T(8,128)}), f32[32,4608]{1,0:T(8,128)}) %reduce-scatter.13.cloned.1.call-update) | async-done | bytes 589840 | tf_op jit(solution)/shard_map/reduce_scatter | solution.py:166
  807.8 212.5 %reduce-scatter.15.cloned.1.call-done = f32[32,4608]{1,0:T(8,128)} async-done(((f32[1024,4608]{1,0:T(8,128)}), f32[32,4608]{1,0:T(8,128)}) %reduce-scatter.15.cloned.1.call-update) | async-done | bytes 589840 | tf_op jit(solution)/shard_map/reduce_scatter | solution.py:167
  1020.3 212.6 %reduce-scatter.17.cloned.1.call-done = f32[144,1024]{1,0:T(8,128)} async-done(((f32[4608,1024]{1,0:T(8,128)}), f32[144,1024]{1,0:T(8,128)}) %reduce-scatter.17.cloned.1.call-update) | async-done | bytes 589840 | tf_op jit(solution)/shard_map/reduce_scatter | solution.py:168
  (118 shorter events, 25.0 us)
Async XLA Ops:
  7.2 21.9 %all-gather.8.cloned.1.call-start = ((), (), s32[]{:S(2)}) async-start(), calls=%async_computation.6 | async-start | bytes 9437184 | tf_op jit(solution)/shard_map/all_gather | solution.py:70
  7.9 35.3 %all-gather.10.cloned.1.call-start = ((), (), s32[]{:S(2)}) async-start(), calls=%async_computation.7 | async-start | bytes 3145728 | tf_op jit(solution)/shard_map/all_gather | solution.py:71
  8.7 58.3 %all-gather.12.cloned.1.call-start = ((), (), s32[]{:S(2)}) async-start(), calls=%async_computation.8 | async-start | bytes 14155776 | tf_op jit(solution)/shard_map/all_gather | solution.py:72
  9.4 82.0 %all-gather.14.cloned.1.call-start = ((), (), s32[]{:S(2)}) async-start(), calls=%async_computation.9 | async-start | bytes 14155776 | tf_op jit(solution)/shard_map/all_gather | solution.py:73
  10.0 2.9 copy-start.21
  10.0 4.8 copy-start.4
  10.0 105.9 %all-gather.16.cloned.1.call-start = ((), (), s32[]{:S(2)}) async-start(), calls=%async_computation.10 | async-start | bytes 14155776 | tf_op jit(solution)/shard_map/all_gather | solution.py:74
  10.6 285.2 %reduce-scatter.19.cloned.1.call-start = ((), (), s32[]{:S(2)}) async-start(), calls=%async_computation.16 | async-start | bytes 540672
  34.8 6.1 copy-start
  34.8 2.7 copy-start.23
  35.4 5.5 collective-permute-start
  133.9 9.2 copy-start.9
  133.9 9.2 copy-start.12
  143.1 8.4 copy-start.19
  151.5 1.6 copy-start.25
  153.1 2.3 copy-start.7
  160.4 275.6 %reduce-scatter.11.cloned.1.call-start = ((), (), s32[]{:S(2)}) async-start(), calls=%async_computation.12 | async-start | bytes 4325376 | tf_op jit(solution)/shard_map/reduce_scatter | solution.py:164
  165.5 429.4 %reduce-scatter.9.cloned.1.call-start = ((), (), s32[]{:S(2)}) async-start(), calls=%async_computation.11 | async-start | bytes 12976128 | tf_op jit(solution)/shard_map/reduce_scatter | solution.py:162
  167.7 3.8 slice-start
  168.1 3.4 slice-start.1
  168.1 3.3 collective-permute-start.1
  171.5 2.2 copy-start.5
  171.5 2.2 copy-start.13
  180.5 627.2 %reduce-scatter.13.cloned.1.call-start = ((), (), s32[]{:S(2)}) async-start(), calls=%async_computation.13 | async-start | bytes 19464192 | tf_op jit(solution)/shard_map/reduce_scatter | solution.py:166
  192.4 827.9 %reduce-scatter.15.cloned.1.call-start = ((), (), s32[]{:S(2)}) async-start(), calls=%async_computation.14 | async-start | bytes 19464192 | tf_op jit(solution)/shard_map/reduce_scatter | solution.py:167
  204.0 1028.9 %reduce-scatter.17.cloned.1.call-start = ((), (), s32[]{:S(2)}) async-start(), calls=%async_computation.15 | async-start | bytes 19464192 | tf_op jit(solution)/shard_map/reduce_scatter | solution.py:168
  216.7 1.6 copy-start.10
  218.3 9.9 copy-start.6
  218.3 9.9 copy-start.14
  218.3 9.9 copy-start.16
  218.3 9.9 copy-start.18
  228.3 51.7 %copy-start.2 = (f32[512,1024]{1,0:T(8,128)S(1)}, f32[512,1024]{1,0:T(8,128)}, u32[]{:S(2)}) copy-start(f32[512,1024]{1,0:T(8,128)} %copy-done.1) | copy-start | bytes 6291460
  (9 other events, 10.8 us)
Sparse Core Ops, SparseCore 0:
  9.5 19.4 all-gather.7
  30.6 11.7 all-gather.9
  43.9 23.0 all-gather.11
  68.4 23.0 all-gather.13
  92.8 23.0 all-gather.15
  160.5 135.2 reduce-scatter.18
  298.8 137.1 reduce-scatter.10
  443.6 151.2 reduce-scatter.8
  601.9 205.8 reduce-scatter.12
  814.6 205.6 reduce-scatter.14
  1027.3 205.6 reduce-scatter.16
where the time goes:
time: 1240 us
  waiting for transfers between devices  1010 us (81%)
  matrix products  133 us (11%)
  blocking collectives  49.6 us (4%)
  between operations  14.8 us (1%)
  local copies, waits for them, and re-layouts  13.5 us (1%)
  other arithmetic  13.3 us (1%)
    reduce_scatter x1, waiting for transfers between devices, local(): lax.psum_scatter(partials[5], ('seq', 'wa'), scatter_dimension=0, tiled=T...  213 us
    reduce_scatter x1, waiting for transfers between devices, local(): lax.psum_scatter(partials[7], ('seq', 'wa'), scatter_dimension=0, tiled=T...  213 us
    reduce_scatter x1, waiting for transfers between devices, local(): lax.psum_scatter(partials[6], ('seq', 'wa'), scatter_dimension=0, tiled=T...  213 us
    reduce_scatter x1, waiting for transfers between devices, local(): lax.psum_scatter(partials[1], ('seq', 'wa'), scatter_dimension=0, tiled=T...  159 us
    reduce_scatter x1, waiting for transfers between devices, local(): lax.psum_scatter(partials[3], ('seq', 'wa'), scatter_dimension=0, tiled=T...  139 us
    dot_general x5, matrix products, left_dot(): lax.dot_general(left, right, (((0,), (0,)), ((), ())), preferred_element_...  46.5 us
    dot_general x5, matrix products, right_dot(): lax.dot_general(left, right, (((1,), (1,)), ((), ())), preferred_element_...  44.7 us
    unnamed x1, blocking collectives  42.6 us
  transfers between devices with their start and end apart: 13, of which 11 were waited for; matrix products, arithmetic and copies ran while one was open for 9% of the time, Pallas kernels for 0%

commit v1 on v0

v1 whole, which is shorter than its diff:
```python
import jax
import jax.numpy as jnp
from jax import lax
from jax.sharding import PartitionSpec as P

epsilon = 1e-05
AXES = ("seq", "wa")


def shifted(value, axis, steps):
    count = lax.axis_size(axis)
    first, last = (max(0, -steps), min(count, count - steps))
    return lax.ppermute(value, axis, [(source, source + steps) for source in range(first, last)])


def partner(value):
    return lax.ppermute(value, "wa", [(0, 1), (1, 0)])


def across(value, bit):
    count = lax.axis_size("seq")
    return lax.ppermute(value, "seq", [(place, place ^ (1 << bit)) for place in range(count)])


def left_dot(left, right):
    return lax.dot_general(
        left, right, (((0,), (0,)), ((), ())), preferred_element_type=jnp.float32
    )


def right_dot(left, right):
    return lax.dot_general(
        left, right, (((1,), (1,)), ((), ())), preferred_element_type=jnp.float32
    )


def plain_dot(left, right):
    return jnp.dot(left, right, preferred_element_type=jnp.float32)


def norm_back(grad_norm, normed, scale, gain):
    inner = grad_norm * gain
    return scale * (inner - normed * jnp.mean(inner * normed, axis=-1, keepdims=True))


def take(value, index, axis):
    return lax.dynamic_index_in_dim(value, index, axis, keepdims=False)


def total(terms):
    result = terms[0].astype(jnp.float32)
    for term in terms[1:]:
        result = result + term.astype(jnp.float32)
    return result


def exchange_sum(value, names, order, coords, move):
    names = list(names)
    terms = [value]
    for name in order:
        axis = names.index(name)
        mine = coords[name]
        send = total([take(term, 1 - mine, axis) for term in terms]).astype(jnp.bfloat16)
        terms = [take(term, mine, axis) for term in terms] + [move(send, name)]
        names.pop(axis)
    return terms


def local(
    tokens,
    cotangent,
    doc_lengths,
    norm_gain,
    in_weight,
    conv_taps,
    out_weight,
    ffn_gain,
    gate_weight,
    up_weight,
    down_weight,
):
    rows, width = tokens.shape
    hidden = down_weight.shape[0]
    chips = lax.axis_size("seq")
    top = chips.bit_length() - 2
    lower = list(range(top))
    chip = lax.axis_index("seq")
    core = lax.axis_index("wa")
    coords = {bit: (chip >> bit) & 1 for bit in range(top + 1)}
    coords["core"] = core

    def move(value, name):
        return partner(value) if name == "core" else across(value, name)

    def ordered(low, high):
        return jnp.where(core == 0, low, high)

    def both(own, axis):
        other = partner(own)
        return ordered(
            jnp.concatenate([own, other], axis=axis), jnp.concatenate([other, own], axis=axis)
        )

    def column_half(weight):
        halves = weight.reshape(weight.shape[0], 2, hidden)
        mine, other = take(halves, core, 1), partner(take(halves, 1 - core, 1))
        return ordered(
            jnp.concatenate([mine, other], axis=0), jnp.concatenate([other, mine], axis=0)
        )

    place = lax.axis_index(AXES) * rows + jnp.arange(rows, dtype=jnp.int32)
    starts = jnp.cumsum(doc_lengths) - doc_lengths
    first = jnp.any(place[:, None] == starts[None, :], axis=1)
    before = jnp.any((place - 1)[:, None] == starts[None, :], axis=1)
    keep_one = jnp.where(first, 0.0, 1.0).astype(jnp.float32)[:, None]
    keep_two = jnp.where(jnp.logical_or(first, before), 0.0, 1.0).astype(jnp.float32)[:, None]
    w_in = both(in_weight, 0)
    small = jnp.concatenate([norm_gain[:, None], ffn_gain[:, None], conv_taps], axis=1)
    small = both(small, 0).astype(jnp.float32)
    gain_one, gain_two, taps = small[:, 0], small[:, 1], small[:, 2:]
    w_out = both(out_weight, 0)
    w_gate = column_half(gate_weight)
    w_up = column_half(up_weight)
    cot_both = jnp.concatenate([cotangent, partner(cotangent)], axis=0)

    resid = tokens.astype(jnp.float32)
    scale_one = lax.rsqrt(jnp.mean(resid * resid, axis=-1, keepdims=True) + epsilon)
    normed_one = resid * scale_one
    norm_in = (normed_one * gain_one).astype(jnp.bfloat16)
    proj = plain_dot(norm_in, w_in)
    b_part = proj[:, :width]
    c_part = proj[:, width : 2 * width]
    x_part = proj[:, 2 * width :]
    mixed_in = b_part * x_part
    previous = shifted(mixed_in[-2:], AXES, 1)
    extended = jnp.concatenate([previous, mixed_in], axis=0)
    back_one = extended[1:-1]
    back_two = extended[:-2]
    conv = (
        taps[:, 0] * mixed_in + keep_one * taps[:, 1] * back_one + keep_two * taps[:, 2] * back_two
    )
    gated = (c_part * conv).astype(jnp.bfloat16)
    hidden_res = resid + plain_dot(gated, w_out)
    scale_two = lax.rsqrt(jnp.mean(hidden_res * hidden_res, axis=-1, keepdims=True) + epsilon)
    normed_two = hidden_res * scale_two
    norm_ffn = (normed_two * gain_two).astype(jnp.bfloat16)

    norm_both = jnp.concatenate([norm_ffn, partner(norm_ffn)], axis=0)
    gate = plain_dot(norm_both, w_gate)
    up_val = plain_dot(norm_both, w_up)
    sigma = jax.nn.sigmoid(gate)
    silu_gate = gate * sigma
    act = (silu_gate * up_val).astype(jnp.bfloat16)
    d_act = right_dot(cot_both, down_weight)
    d_up = (d_act * silu_gate).astype(jnp.bfloat16)
    d_gate = (d_act * up_val * sigma * (1.0 + gate * (1.0 - sigma))).astype(jnp.bfloat16)

    bits = list(range(top, -1, -1))

    def spread(grad, names):
        return grad.astype(jnp.bfloat16).reshape([2] * len(names) + [-1, grad.shape[1]])

    turn = [lower[step % top :] + lower[: step % top] for step in range(3)]
    down_terms = exchange_sum(
        spread(left_dot(act, cot_both), bits[1:]), bits[1:], turn[2], coords, move
    )
    gate_terms = exchange_sum(
        spread(left_dot(norm_both, d_gate), bits), bits, turn[0] + [top], coords, move
    )
    up_terms = exchange_sum(
        spread(left_dot(norm_both, d_up), bits), bits, turn[1] + [top], coords, move
    )

    def finish_columns(terms):
        mine = total(terms)
        mine = mine.reshape(2, mine.shape[0] // 2, mine.shape[1])
        kept, other = take(mine, core, 0), partner(take(mine, 1 - core, 0))
        return ordered(
            jnp.concatenate([kept, other], axis=1), jnp.concatenate([other, kept], axis=1)
        )

    gate_out = finish_columns(gate_terms)
    up_out = finish_columns(up_terms)
    part = total(down_terms)
    pairs = [
        (place * 2 + side, (place ^ (1 << top)) * 2 + side)
        for place in range(chips)
        for side in range(2)
        if (place >> top) & 1 != side
    ]
    part = part + lax.ppermute(part.astype(jnp.bfloat16), AXES, pairs).astype(jnp.float32)
    part = part.reshape(2, part.shape[0] // 2, part.shape[1])
    down_out = jnp.where(
        coords[top] == core, take(part, core, 0), partner(take(part, 1 - core, 0))
    )

    d_norm_both = right_dot(d_gate, w_gate) + right_dot(d_up, w_up)
    d_norm_ffn = d_norm_both[:rows] + partner(d_norm_both[rows:])
    ffn_both = plain_dot(act, down_weight)
    block_out = (hidden_res + ffn_both[:rows] + partner(ffn_both[rows:])).astype(jnp.bfloat16)
    gain_two_grad = jnp.sum(d_norm_ffn * normed_two, axis=0)
    d_hidden = cotangent.astype(jnp.float32) + norm_back(
        d_norm_ffn, normed_two, scale_two, gain_two
    )
    d_branch = d_hidden.astype(jnp.bfloat16)
    out_grad = left_dot(gated, d_branch)
    d_gated = right_dot(d_branch, w_out)
    d_c = d_gated * conv
    d_conv = d_gated * c_part
    tap_terms = [
        jnp.sum(d_conv * mixed_in, axis=0),
        jnp.sum(keep_one * d_conv * back_one, axis=0),
        jnp.sum(keep_two * d_conv * back_two, axis=0),
    ]
    along_one = keep_one * d_conv * taps[:, 1]
    along_two = keep_two * d_conv * taps[:, 2]
    zero_row = jnp.zeros((1, width), jnp.float32)
    d_mixed = (
        taps[:, 0] * d_conv
        + jnp.concatenate([along_one[1:], zero_row], axis=0)
        + jnp.concatenate([along_two[2:], zero_row, zero_row], axis=0)
    )
    head_grad = jnp.concatenate([along_two[0:1], along_one[0:1] + along_two[1:2]], axis=0)
    returned = shifted(head_grad, AXES, -1)
    d_mixed = jnp.concatenate([d_mixed[:-2], d_mixed[-2:] + returned], axis=0)
    d_proj = jnp.concatenate([d_mixed * x_part, d_c, d_mixed * b_part], axis=1).astype(jnp.bfloat16)
    in_grad = left_dot(norm_in, d_proj)
    d_norm_in = right_dot(d_proj, w_in)
    gain_one_grad = jnp.sum(d_norm_in * normed_one, axis=0)
    input_grad = (d_hidden + norm_back(d_norm_in, normed_one, scale_one, gain_one)).astype(
        jnp.bfloat16
    )
    vectors = jnp.stack([gain_one_grad, gain_two_grad] + tap_terms, axis=0).T
    vectors = jnp.pad(vectors, ((0, 0), (0, 128 - vectors.shape[1])))
    joint = jnp.concatenate([in_grad, out_grad, vectors], axis=1)
    third = joint.shape[1] // 3
    names = bits + ["core"]
    joint_out = jnp.concatenate(
        [
            total(
                exchange_sum(
                    spread(joint[:, step * third : (step + 1) * third], names),
                    names,
                    ["core"] + turn[step] + [top],
                    coords,
                    move,
                )
            )
            for step in range(3)
        ],
        axis=1,
    )
    in_out = joint_out[:, : 3 * width]
    out_out = joint_out[:, 3 * width : 4 * width]
    vectors_out = joint_out[:, 4 * width :]
    return (
        block_out,
        input_grad,
        vectors_out[:, 0],
        in_out,
        vectors_out[:, 2:5],
        out_out,
        vectors_out[:, 1],
        gate_out,
        up_out,
        down_out,
    )


def solution(mesh):
    placed = (
        P(AXES, None),
        P(AXES, None),
        P(),
        P("wa"),
        P("wa", None),
        P("wa", None),
        P("wa", None),
        P("wa"),
        P("wa", None),
        P("wa", None),
        P("wa", None),
    )
    return jax.shard_map(
        local,
        mesh=mesh,
        in_specs=placed,
        out_specs=(
            P(AXES, None),
            P(AXES, None),
            P(AXES),
            P(AXES, None),
            P(AXES, None),
            P(AXES, None),
            P(AXES),
            P(AXES, None),
            P(AXES, None),
            P(AXES, None),
        ),
        check_vma=False,
    )
```

time: 1240 us -> 373 us (0.30)
  waiting for transfers between devices: 1010 us -> 74.2 us
  starting transfers between devices: 4.11 us -> 73.2 us
  blocking collectives: 49.6 us -> 0 us
  local copies, waits for them, and re-layouts: 13.5 us -> 57.7 us
  other arithmetic: 13.3 us -> 40.6 us
  matrix products: 133 us -> 120 us
  between operations: 14.8 us -> 1.98 us
    reduce_scatter x5 -> x0, waiting for transfers between devices: 936 us -> none  [the longest x1 213 us: local(): lax.psum_scatter(partials[5], ('seq', 'wa'), scatter_dimension=0, tiled=T...]
    ppermute x0 -> x39, waiting for transfers between devices: none -> 73.2 us  [the longest x23 73.2 us: across(): lax.ppermute(value, 'seq', [(place, place ^ 1 << bit) for place in range(...]
    ppermute x0 -> x39, starting transfers between devices: none -> 69.2 us  [the longest x15 38.5 us: partner(): return lax.ppermute(value, 'wa', [(0, 1), (1, 0)])]
    all_gather x5 -> x0, waiting for transfers between devices: 58.9 us -> none  [the longest x1 18.9 us: local(): lax.all_gather(shards[5], 'wa', axis=0, tiled=True)]
    unnamed x1 -> x0, blocking collectives: 42.6 us -> none
    dynamic_slice x0 -> x5, local copies, waits for them, and re-layouts: none -> 22.4 us  [take(): return lax.dynamic_index_in_dim(value, index, axis, keepdims=False)]
    unnamed x12 -> x0, waiting for transfers between devices: 16 us -> none
    dot_general x5, matrix products: 46.5 us -> 30.9 us  [left_dot(): lax.dot_general(left, right, (((0,), (0,)), ((), ())), preferred_element_...]
  transfers between devices with their start and end apart: 13 -> 41, of which waited for: 11 -> 13; matrix products, arithmetic and copies ran while one was open for 9% -> 47% of each run, Pallas kernels for 0% -> 0%
where the time goes in v1:
time: 373 us; the launch traced here: 367 us
  matrix products  120 us (32%)
  waiting for transfers between devices  74.2 us (20%)
  starting transfers between devices  73.2 us (20%)
  local copies, waits for them, and re-layouts  57.7 us (15%)
  other arithmetic  40.6 us (11%)
    ppermute x23, waiting for transfers between devices, across(): lax.ppermute(value, 'seq', [(place, place ^ 1 << bit) for place in range(...  73.2 us
    dot_general x5, matrix products, plain_dot(): return jnp.dot(left, right, preferred_element_type=jnp.float32)  48.5 us
    dot_general x5, matrix products, right_dot(): lax.dot_general(left, right, (((1,), (1,)), ((), ())), preferred_element_...  40.3 us
    ppermute x15, starting transfers between devices, partner(): return lax.ppermute(value, 'wa', [(0, 1), (1, 0)])  38.5 us
    dot_general x5, matrix products, left_dot(): lax.dot_general(left, right, (((0,), (0,)), ((), ())), preferred_element_...  30.9 us
    ppermute x23, starting transfers between devices, across(): lax.ppermute(value, 'seq', [(place, place ^ 1 << bit) for place in range(...  29.1 us
    unnamed x94, local copies, waits for them, and re-layouts  22.5 us
    dynamic_slice x5, local copies, waits for them, and re-layouts, take(): return lax.dynamic_index_in_dim(value, index, axis, keepdims=False)  22.4 us
  transfers between devices with their start and end apart: 41, of which 13 were waited for; matrix products, arithmetic and copies ran while one was open for 47% of the time, Pallas kernels for 0%

profile of v1, /device:TPU:0, one launch (start us, length us, event | category | flops | bytes accessed | tf_op | source)
XLA Modules:
  0.0 367.4 jit_solution(13056039482774602255)
XLA Ops:
  3.8 6.6 %copy.161 = bf16[512,4608]{0,1:T(8,128)(2,1)} copy(bf16[512,4608]{1,0:T(8,128)(2,1)} %param.19) | data formatting | bytes 9437184 | tf_op args[8]
  10.4 6.7 %copy.164 = bf16[512,4608]{0,1:T(8,128)(2,1)} copy(bf16[512,4608]{1,0:T(8,128)(2,1)} %param.20) | data formatting | bytes 9437184 | tf_op args[9]
  17.1 6.8 %constant_dynamic-slice_fusion.6 = (bf16[512,1,2304]{0,2,1:T(8,128)(2,1)}, bf16[512,1,2304]{0,2,1:T(8,128)(2,1)}, bf16[512,1,2304]{0,2,1:T(8,128)(2,1)}, bf16[512,1,2304]{0,2,1:T(8,128)(2,1)S(1)}) fusion(bf16[512,2,2304]{0,2,1:T(8,128)(2,1)} %bitcast.387, s32[]{:T(128)S(6)} %select_n.290, s32[]{:T(128)S(6)} %select_n.291, bf16[512,2,2304]{0,2,1:T(8,128)(2,1)} %bitcast.386), kind=kLoop, calls=%fused_computation.192 | loop fusion | bytes 18874376 | tf_op jit(solution)/shard_map/jit(dynamic_index_in_dim)/dynamic_slice | solution.py:47
  23.9 4.4 %copy.166 = bf16[512,1,2304]{2,0,1:T(8,128)(2,1)} copy(bf16[512,1,2304]{0,2,1:T(8,128)(2,1)} %get-tuple-element.85) | data formatting | bytes 4718592 | tf_op jit(solution)/shard_map/jit(dynamic_index_in_dim)/dynamic_slice | solution.py:47
  31.8 4.3 %copy.165 = bf16[512,1,2304]{2,0,1:T(8,128)(2,1)} copy(bf16[512,1,2304]{0,2,1:T(8,128)(2,1)} %get-tuple-element.84) | data formatting | bytes 4718592 | tf_op jit(solution)/shard_map/jit(dynamic_index_in_dim)/dynamic_slice | solution.py:47
  36.2 4.3 %copy.163 = bf16[512,1,2304]{2,0,1:T(8,128)(2,1)} copy(bf16[512,1,2304]{0,2,1:T(8,128)(2,1)} %get-tuple-element.109) | data formatting | bytes 4718592 | tf_op jit(solution)/shard_map/jit(dynamic_index_in_dim)/dynamic_slice | solution.py:47
  43.2 7.5 %fusion.29 = f32[512,3072]{1,0:T(8,128)S(1)} fusion(bf16[512,3072]{1,0:T(8,128)(2,1)} %collective-permute-done.1, bf16[512,3072]{1,0:T(8,128)(2,1)} %param.15, pred[]{:T(512)S(6)} %eq.14, bf16[512,1024]{1,0:T(8,128)(2,1)} %param.11, f32[1024]{0:T(1024)S(1)} %bitcast.450, f32[512]{0:T(512)S(1)} %add_rsqrt_fusion.1), kind=kOutput, calls=%fused_computation.95 | convolution fusion | flops 3251634176 | bytes 13637633 | tf_op jit(solution)/shard_map/dot_general | solution.py:38
  51.2 2.8 collective-permute-start.2
  58.6 3.7 multiply_reduce_fusion.5
  65.0 7.5 %fusion.69 = f32[1024,2304]{1,0:T(8,128)} fusion(bf16[1024,1024]{1,0:T(8,128)(2,1)S(1)} %constant_dynamic-update-slice_fusion, bf16[2304,1024]{1,0:T(8,128)(2,1)S(1)} %bitcast.456), kind=kOutput, calls=%fused_computation.226 | convolution fusion | flops 4831838208 | bytes 16252928 | tf_op jit(solution)/shard_map/dot_general | solution.py:32
  72.6 10.0 %fusion.31 = f32[1024,2304]{1,0:T(8,128)} fusion(bf16[512,2304]{1,0:T(8,128)(2,1)} %collective-permute-done.6, bf16[512,2304]{1,0:T(8,128)(2,1)S(1)} %bitcast.433, pred[]{:T(512)S(6)} %eq.14, bf16[512,1024]{1,0:T(8,128)(2,1)S(1)} %collective-permute-done.4, bf16[512,1024]{1,0:T(8,128)(2,1)S(1)} %multiply_convert_fusion.6), kind=kOutput, calls=%fused_computation.97 | convolution fusion | flops 4857266176 | bytes 16252929 | tf_op jit(solution)/shard_map/dot_general | solution.py:38
  82.6 18.3 %multiply_convert_fusion.1 = (bf16[1024,2304]{1,0:T(8,128)(2,1)}, bf16[1024,2304]{1,0:T(8,128)(2,1)}, bf16[1024,2304]{1,0:T(8,128)(2,1)}) fusion(f32[1024,2304]{1,0:T(8,128)} %fusion.69, f32[1024,2304]{1,0:T(8,128)} %fusion.31, bf16[512,2304]{1,0:T(8,128)(2,1)} %collective-permute-done.5, bf16[512,2304]{1,0:T(8,128)(2,1)} %bitcast.435, pred[]{:T(512)S(6)} %eq.14, ...), kind=kOutput, calls=%fused_computation.1 | convolution fusion | flops 4892655616 | bytes 39845888 | tf_op jit(solution)/shard_map/dot_general | solution.py:38
  100.9 8.2 %convolution_convert_fusion.1 = bf16[2304,1024]{1,0:T(8,128)(2,1)S(1)} fusion(bf16[1024,2304]{1,0:T(8,128)(2,1)} %get-tuple-element.76, bf16[1024,1024]{1,0:T(8,128)(2,1)} %copy-done.22), kind=kOutput, calls=%fused_computation.9 | convolution fusion | flops 4834197504 | bytes 11534336 | tf_op jit(solution)/shard_map/dot_general | solution.py:26
  109.1 9.0 %fusion.68 = f32[1024,1024]{1,0:T(8,128)S(1)} fusion(bf16[1024,2304]{1,0:T(8,128)(2,1)S(1)} %copy-done.30, bf16[2304,1024]{1,0:T(8,128)(2,1)} %param.21), kind=kOutput, calls=%fused_computation.225 | convolution fusion | flops 4831838208 | bytes 13631488 | tf_op jit(solution)/shard_map/dot_general | solution.py:38
  122.2 9.6 %fusion.30 = f32[1024,1024]{1,0:T(8,128)} fusion(bf16[1024,2304]{1,0:T(8,128)(2,1)S(1)} %bitcast.460, bf16[512,2304]{1,0:T(8,128)(2,1)} %collective-permute-done.6, bf16[512,2304]{1,0:T(8,128)(2,1)S(1)} %bitcast.434, pred[]{:T(512)S(6)} %eq.14), kind=kOutput, calls=%fused_computation.96 | convolution fusion | flops 4853071872 | bytes 13631489 | tf_op jit(solution)/shard_map/dot_general | solution.py:32
  131.8 10.1 %convolution_add_fusion = f32[1024,1024]{1,0:T(8,128)S(1)} fusion(f32[1024,1024]{1,0:T(8,128)} %fusion.30, bf16[1024,2304]{1,0:T(8,128)(2,1)} %get-tuple-element.74, bf16[512,2304]{1,0:T(8,128)(2,1)} %collective-permute-done.5, bf16[512,2304]{1,0:T(8,128)(2,1)S(1)} %bitcast.436, pred[]{:T(512)S(6)} %eq.14), kind=kOutput, calls=%fused_computation.70 | convolution fusion | flops 4854120448 | bytes 17825792 | tf_op jit(solution)/shard_map/dot_general | solution.py:32
  143.8 8.2 %convolution_convert_fusion.2 = bf16[1024,2304]{1,0:T(8,128)(2,1)S(1)} fusion(bf16[1024,2304]{1,0:T(8,128)(2,1)} %get-tuple-element.75, bf16[512,1024]{1,0:T(8,128)(2,1)S(1)} %copy-done.29, bf16[512,1024]{1,0:T(8,128)(2,1)S(1)} %copy-done.18), kind=kOutput, calls=%fused_computation.10 | convolution fusion | flops 4838391808 | bytes 11534336 | tf_op jit(solution)/shard_map/dot_general | solution.py:26
  155.6 5.8 %convolution_convert_fusion.3 = bf16[1024,2304]{1,0:T(8,128)(2,1)S(1)} fusion(bf16[1024,2304]{1,0:T(8,128)(2,1)S(1)} %bitcast.458, bf16[512,1024]{1,0:T(8,128)(2,1)S(1)} %copy-done.29, bf16[512,1024]{1,0:T(8,128)(2,1)S(1)} %copy-done.18), kind=kOutput, calls=%fused_computation.11 | convolution fusion | flops 4838391808 | bytes 11534336 | tf_op jit(solution)/shard_map/dot_general | solution.py:26
  168.0 4.3 %multiply_add_fusion = (f32[512,1024]{1,0:T(8,128)S(1)}, bf16[512,1024]{1,0:T(8,128)(2,1)}) fusion(bf16[512,1024]{1,0:T(8,128)(2,1)S(1)} %copy-done.10, f32[512,1024]{1,0:T(8,128)S(1)} %get-tuple-element.105, f32[512]{0:T(512)S(1)} %broadcast_multiply_fusion.1, f32[1024]{0:T(1024)S(1)} %bitcast.443, f32[512]{0:T(512)S(1)} %add_rsqrt_fusion, ...), kind=kLoop, calls=%fused_computation.60 | loop fusion | flops 5767168 | bytes 14688256 | tf_op jit(solution)/shard_map/add | solution.py:202
  172.3 5.1 %multiply_reduce_fusion = (bf16[1024]{0:T(1024)(128)(2,1)S(1)}, bf16[1024]{0:T(1024)(128)(2,1)S(1)}, bf16[1024]{0:T(1024)(128)(2,1)S(1)}, f32[512,1024]{1,0:T(8,128)S(1)}, bf16[512,1024]{1,0:T(8,128)(2,1)S(1)}) fusion(f32[512,1024]{1,0:T(8,128)S(1)} %copy-done.2, f32[2,1024]{1,0:T(2,128)S(1)} %collective-permute-done.2, f32[512]{0:T(512)S(1)} %get-tuple-element.103, ...), kind=kOutput, calls=%fused_computation.52 | convolution fusion | flops 1090515968 | bytes 13649921 | tf_op jit(solution)/shard_map/dot_general | solution.py:32
  187.3 7.9 %fusion.17 = (bf16[1024]{0:T(1024)(128)(2,1)S(1)}, f32[512]{0:T(512)S(1)}, f32[512,1024]{1,0:T(8,128)}) fusion(bf16[512,1024]{1,0:T(8,128)(2,1)S(1)} %copy-done.12, f32[512]{0:T(512)S(1)} %add_rsqrt_fusion.1, f32[1024]{0:T(1024)S(1)} %bitcast.451, bf16[512,3072]{1,0:T(8,128)(2,1)} %collective-permute-done.1, bf16[512,3072]{1,0:T(8,128)(2,1)S(1)} %copy-done.25, ...), kind=kOutput, calls=%fused_computation.42 | convolution fusion | flops 3262642688 | bytes 12593153 | tf_op jit(solution)/shard_map/dot_general | solution.py:32
  195.2 6.1 %convolution_convert_fusion = bf16[1024,3072]{1,0:T(8,128)(2,1)} fusion(bf16[512,1024]{1,0:T(8,128)(2,1)S(1)} %get-tuple-element.78, bf16[512,1024]{1,0:T(8,128)(2,1)S(1)} %get-tuple-element.86, bf16[512,1024]{1,0:T(8,128)(2,1)S(1)} %get-tuple-element.77, bf16[512,1024]{1,0:T(8,128)(2,1)S(1)} %copy-done.12, f32[1024]{0:T(1024)S(1)} %bitcast.452, ...), kind=kOutput, calls=%fused_computation.8 | convolution fusion | flops 3235905536 | bytes 10491904 | tf_op jit(solution)/shard_map/dot_general | solution.py:26
  201.6 3.9 %fusion.65 = (bf16[1024,1408]{1,0:T(8,128)(2,1)S(1)}, bf16[1024,1408]{1,0:T(8,128)(2,1)S(1)}, bf16[1024,1408]{1,0:T(8,128)(2,1)S(1)}) fusion(bf16[1024,3072]{1,0:T(8,128)(2,1)} %convolution_convert_fusion, bf16[1024,5]{1,0:T(8,128)(2,1)S(1)} %bitcast.440, bf16[1024,1024]{1,0:T(8,128)(2,1)} %convolution_convert_fusion.4), kind=kLoop, calls=%fused_computation.222 | loop fusion | flops 12976128 | bytes 22816768 | tf_op jit(solution)/shard_map/slice | solution.py:242
  205.8 33.0 %collective-permute-start.16 = (bf16[2,2,2,2,32,1408]{5,4,0,3,2,1:T(8,128)(2,1)S(1)}, bf16[2,2,2,2,32,1408]{5,4,0,3,2,1:T(8,128)(2,1)S(1)}, u32[]{:S(2)}, u32[]{:S(2)}) collective-permute-start(bf16[2,2,2,2,32,1408]{5,4,0,3,2,1:T(8,128)(2,1)S(1)} %copy.176), channel_id=1, source_target_pairs={{0,1},{1,0},{2,3},{3,2},{4,5},{5,4},{6,7},{7,6},{8,9},{9,8},{10,11... | collective-permute-start | bytes 4325384 | tf_op jit(solution)/shard_map/ppermute | solution.py:17
  249.1 20.8 %collective-permute-done.37 = bf16[2,288,1024]{2,1,0:T(8,128)(2,1)S(1)} collective-permute-done((bf16[2,288,1024]{2,1,0:T(8,128)(2,1)S(1)}, bf16[2,288,1024]{2,1,0:T(8,128)(2,1)S(1)}, u32[]{:S(2)}, u32[]{:S(2)}) %collective-permute-start.37) | collective-permute-done | bytes 1179680 | tf_op jit(solution)/shard_map/ppermute | solution.py:22
  282.4 6.9 %collective-permute-done.38 = bf16[288,1024]{1,0:T(8,128)(2,1)S(1)} collective-permute-done((bf16[288,1024]{1,0:T(8,128)(2,1)S(1)}, bf16[288,1024]{1,0:T(8,128)(2,1)S(1)}, u32[]{:S(2)}, u32[]{:S(2)}) %collective-permute-start.38) | collective-permute-done | bytes 589856 | tf_op jit(solution)/shard_map/ppermute | solution.py:22
  295.8 3.6 collective-permute-start.34
  300.7 6.0 %collective-permute-done.17 = bf16[2,2,2,32,1408]{4,3,2,1,0:T(8,128)(2,1)S(1)} collective-permute-done((bf16[2,2,2,32,1408]{4,3,2,1,0:T(8,128)(2,1)S(1)}, bf16[2,2,2,32,1408]{4,3,2,1,0:T(8,128)(2,1)S(1)}, u32[]{:S(2)}, u32[]{:S(2)}) %collective-permute-start.17) | collective-permute-done | bytes 720928 | tf_op jit(solution)/shard_map/ppermute | solution.py:22
  310.6 10.4 %collective-permute-done.12 = bf16[2,2,2,32,1408]{4,3,2,1,0:T(8,128)(2,1)S(1)} collective-permute-done((bf16[2,2,2,32,1408]{4,3,2,1,0:T(8,128)(2,1)S(1)}, bf16[2,2,2,32,1408]{4,3,2,1,0:T(8,128)(2,1)S(1)}, u32[]{:S(2)}, u32[]{:S(2)}) %collective-permute-start.12) | collective-permute-done | bytes 720928 | tf_op jit(solution)/shard_map/ppermute | solution.py:22
  321.2 13.0 %collective-permute-done.34 = bf16[64,2304]{1,0:T(8,128)(2,1)S(1)} collective-permute-done((bf16[64,2304]{1,0:T(8,128)(2,1)S(1)}, bf16[64,2304]{1,0:T(8,128)(2,1)S(1)}, u32[]{:S(2)}, u32[]{:S(2)}) %collective-permute-start.34) | collective-permute-done | bytes 294944 | tf_op jit(solution)/shard_map/ppermute | solution.py:22
  348.4 3.0 collective-permute-start.25
  351.5 7.9 %collective-permute-done.20 = bf16[32,1408]{1,0:T(8,128)(2,1)S(1)} collective-permute-done((bf16[32,1408]{1,0:T(8,128)(2,1)S(1)}, bf16[32,1408]{1,0:T(8,128)(2,1)S(1)}, u32[]{:S(2)}, u32[]{:S(2)}) %collective-permute-start.20) | collective-permute-done | bytes 90144 | tf_op jit(solution)/shard_map/ppermute | solution.py:22
  (262 shorter events, 99.6 us)
Async XLA Ops:
  0.6 42.6 %collective-permute-start.1 = (bf16[512,3072]{1,0:T(8,128)(2,1)}, bf16[512,3072]{1,0:T(8,128)(2,1)}, u32[]{:S(2)}, u32[]{:S(2)}) collective-permute-start(bf16[512,3072]{1,0:T(8,128)(2,1)} %param.15), channel_id=1, source_target_pairs={{0,1},{1,0},{2,3},{3,2},{4,5},{5,4},{6,7},{7,6},{8,9},{9,8},{10,11... | collective-permute-start | bytes 9437192 | tf_op jit(solution)/shard_map/ppermute | solution.py:17
  3.2 39.8 %collective-permute-start = (bf16[512,5]{0,1:T(8,128)(2,1)S(1)}, bf16[512,5]{0,1:T(8,128)(2,1)S(1)}, u32[]{:S(2)}, u32[]{:S(2)}) collective-permute-start(bf16[512,5]{0,1:T(8,128)(2,1)S(1)} %pad_maximum_fusion.9), channel_id=1, source_target_pairs={{0,1},{1,0},{2,3},{3,2},{4,5},{5,4},{6,7},{7,6},{8,9},{9,8},{10,11... | collective-permute-start | bytes 15368 | tf_op jit(solution)/shard_map/ppermute | solution.py:17
  3.3 54.6 %collective-permute-start.3 = (bf16[512,1024]{1,0:T(8,128)(2,1)}, bf16[512,1024]{1,0:T(8,128)(2,1)}, u32[]{:S(2)}, u32[]{:S(2)}) collective-permute-start(bf16[512,1024]{1,0:T(8,128)(2,1)} %param.17), channel_id=1, source_target_pairs={{0,1},{1,0},{2,3},{3,2},{4,5},{5,4},{6,7},{7,6},{8,9},{9,8},{10,11... | collective-permute-start | bytes 3145736 | tf_op jit(solution)/shard_map/ppermute | solution.py:17
  28.3 44.2 %collective-permute-start.6 = (bf16[512,2304]{1,0:T(8,128)(2,1)}, bf16[512,2304]{1,0:T(8,128)(2,1)}, u32[]{:S(2)}, u32[]{:S(2)}) collective-permute-start(bf16[512,2304]{1,0:T(8,128)(2,1)} %bitcast.432), channel_id=1, source_target_pairs={{0,1},{1,0},{2,3},{3,2},{4,5},{5,4},{6,7},{7,6},{8,9},{9,8},{10,11... | collective-permute-start | bytes 7077896 | tf_op jit(solution)/shard_map/ppermute | solution.py:17
  28.4 25.6 %collective-permute-start.8 = (bf16[512,1024]{1,0:T(8,128)(2,1)S(1)}, bf16[512,1024]{1,0:T(8,128)(2,1)}, u32[]{:S(2)}, u32[]{:S(2)}) collective-permute-start(bf16[512,1024]{1,0:T(8,128)(2,1)S(1)} %copy-done.10), channel_id=1, source_target_pairs={{0,1},{1,0},{2,3},{3,2},{4,5},{5,4},{6,7},{7,6},{8,9},{9,8},{10,11... | collective-permute-start | bytes 3145736 | tf_op jit(solution)/shard_map/ppermute | solution.py:17
  43.1 39.5 %collective-permute-start.5 = (bf16[512,2304]{1,0:T(8,128)(2,1)}, bf16[512,2304]{1,0:T(8,128)(2,1)}, u32[]{:S(2)}, u32[]{:S(2)}) collective-permute-start(bf16[512,2304]{1,0:T(8,128)(2,1)} %bitcast.437), channel_id=1, source_target_pairs={{0,1},{1,0},{2,3},{3,2},{4,5},{5,4},{6,7},{7,6},{8,9},{9,8},{10,11... | collective-permute-start | bytes 7077896 | tf_op jit(solution)/shard_map/ppermute | solution.py:17
  119.8 119.4 %collective-permute-start.36 = (bf16[2,2,288,1024]{3,2,0,1:T(8,128)(2,1)}, bf16[2,2,288,1024]{3,2,0,1:T(8,128)(2,1)}, u32[]{:S(2)}, u32[]{:S(2)}) collective-permute-start(bf16[2,2,288,1024]{3,2,0,1:T(8,128)(2,1)} %copy_bitcast_fusion), channel_id=1, source_target_pairs={{0,8},{2,10},{4,12},{6,14},{8,0},{10,2},{12,4},{14,6},{16,24},{18,... | collective-permute-start | bytes 7077896 | tf_op jit(solution)/shard_map/ppermute | solution.py:22
  142.2 23.5 %collective-permute-start.9 = (f32[512,1024]{1,0:T(8,128)S(1)}, f32[512,1024]{1,0:T(8,128)S(1)}, u32[]{:S(2)}, u32[]{:S(2)}) collective-permute-start(f32[512,1024]{1,0:T(8,128)S(1)} %slice.148), channel_id=1, source_target_pairs={{0,1},{1,0},{2,3},{3,2},{4,5},{5,4},{6,7},{7,6},{8,9},{9,8},{10,11... | collective-permute-start | bytes 6291464 | tf_op jit(solution)/shard_map/ppermute | solution.py:17
  142.8 23.8 %collective-permute-start.7 = (f32[512,1024]{1,0:T(8,128)S(1)}, f32[512,1024]{1,0:T(8,128)}, u32[]{:S(2)}, u32[]{:S(2)}) collective-permute-start(f32[512,1024]{1,0:T(8,128)S(1)} %slice.146), channel_id=1, source_target_pairs={{0,1},{1,0},{2,3},{3,2},{4,5},{5,4},{6,7},{7,6},{8,9},{9,8},{10,11... | collective-permute-start | bytes 6291464 | tf_op jit(solution)/shard_map/ppermute | solution.py:17
  154.7 87.2 %collective-permute-start.31 = (bf16[2,2,2,64,2304]{4,3,2,1,0:T(8,128)(2,1)}, bf16[2,2,2,64,2304]{4,3,2,1,0:T(8,128)(2,1)}, u32[]{:S(2)}, u32[]{:S(2)}) collective-permute-start(bf16[2,2,2,64,2304]{4,3,2,1,0:T(8,128)(2,1)} %dynamic-slice_bitcast_fusion), channel_id=1, source_target_pairs={{0,4},{2,6},{4,0},{6,2},{8,12},{10,14},{12,8},{14,10},{16,20},{18,... | collective-permute-start | bytes 7077896 | tf_op jit(solution)/shard_map/ppermute | solution.py:22
  164.3 81.0 %collective-permute-start.26 = (bf16[2,2,2,64,2304]{4,3,2,1,0:T(8,128)(2,1)}, bf16[2,2,2,64,2304]{4,3,2,1,0:T(8,128)(2,1)}, u32[]{:S(2)}, u32[]{:S(2)}) collective-permute-start(bf16[2,2,2,64,2304]{4,3,2,1,0:T(8,128)(2,1)} %dynamic-slice_bitcast_fusion.1), channel_id=1, source_target_pairs={{0,2},{2,0},{4,6},{6,4},{8,10},{10,8},{12,14},{14,12},{16,18},{18,... | collective-permute-start | bytes 7077896 | tf_op jit(solution)/shard_map/ppermute | solution.py:22
  205.8 74.0 %collective-permute-start.16 = (bf16[2,2,2,2,32,1408]{5,4,0,3,2,1:T(8,128)(2,1)S(1)}, bf16[2,2,2,2,32,1408]{5,4,0,3,2,1:T(8,128)(2,1)S(1)}, u32[]{:S(2)}, u32[]{:S(2)}) collective-permute-start(bf16[2,2,2,2,32,1408]{5,4,0,3,2,1:T(8,128)(2,1)S(1)} %copy.176), channel_id=1, source_target_pairs={{0,1},{1,0},{2,3},{3,2},{4,5},{5,4},{6,7},{7,6},{8,9},{9,8},{10,11... | collective-permute-start | bytes 4325384 | tf_op jit(solution)/shard_map/ppermute | solution.py:17
  239.1 41.0 %collective-permute-start.21 = (bf16[2,2,2,2,32,1408]{5,4,0,3,2,1:T(8,128)(2,1)S(1)}, bf16[2,2,2,2,32,1408]{5,4,0,3,2,1:T(8,128)(2,1)S(1)}, u32[]{:S(2)}, u32[]{:S(2)}) collective-permute-start(bf16[2,2,2,2,32,1408]{5,4,0,3,2,1:T(8,128)(2,1)S(1)} %copy.182), channel_id=1, source_target_pairs={{0,1},{1,0},{2,3},{3,2},{4,5},{5,4},{6,7},{7,6},{8,9},{9,8},{10,11... | collective-permute-start | bytes 4325384 | tf_op jit(solution)/shard_map/ppermute | solution.py:17
  241.1 28.8 %collective-permute-start.37 = (bf16[2,288,1024]{2,1,0:T(8,128)(2,1)S(1)}, bf16[2,288,1024]{2,1,0:T(8,128)(2,1)S(1)}, u32[]{:S(2)}, u32[]{:S(2)}) collective-permute-start(bf16[2,288,1024]{2,1,0:T(8,128)(2,1)S(1)} %fusion.7), channel_id=1, source_target_pairs={{0,2},{2,0},{4,6},{6,4},{8,10},{10,8},{12,14},{14,12},{16,18},{18,... | collective-permute-start | bytes 3538952 | tf_op jit(solution)/shard_map/ppermute | solution.py:22
  243.6 29.3 %collective-permute-start.32 = (bf16[2,2,64,2304]{3,2,0,1:T(8,128)(2,1)S(1)}, bf16[2,2,64,2304]{3,2,0,1:T(8,128)(2,1)}, u32[]{:S(2)}, u32[]{:S(2)}) collective-permute-start(bf16[2,2,64,2304]{3,2,0,1:T(8,128)(2,1)S(1)} %copy.192), channel_id=1, source_target_pairs={{0,8},{2,10},{4,12},{6,14},{8,0},{10,2},{12,4},{14,6},{16,24},{18,... | collective-permute-start | bytes 3538952 | tf_op jit(solution)/shard_map/ppermute | solution.py:22
  248.0 28.8 %collective-permute-start.27 = (bf16[2,2,64,2304]{3,2,0,1:T(8,128)(2,1)}, bf16[2,2,64,2304]{3,2,0,1:T(8,128)(2,1)}, u32[]{:S(2)}, u32[]{:S(2)}) collective-permute-start(bf16[2,2,64,2304]{3,2,0,1:T(8,128)(2,1)} %copy.189), channel_id=1, source_target_pairs={{0,4},{2,6},{4,0},{6,2},{8,12},{10,14},{12,8},{14,10},{16,20},{18,... | collective-permute-start | bytes 3538952 | tf_op jit(solution)/shard_map/ppermute | solution.py:22
  269.9 11.7 %collective-permute-start.11 = (bf16[2,2,2,2,32,1408]{5,4,3,2,1,0:T(8,128)(2,1)S(1)}, bf16[2,2,2,2,32,1408]{5,4,3,2,1,0:T(8,128)(2,1)S(1)}, u32[]{:S(2)}, u32[]{:S(2)}) collective-permute-start(bf16[2,2,2,2,32,1408]{5,4,3,2,1,0:T(8,128)(2,1)S(1)} %dynamic-slice_bitcast_fusion.4), channel_id=1, source_target_pairs={{0,1},{1,0},{2,3},{3,2},{4,5},{5,4},{6,7},{7,6},{8,9},{9,8},{10,11... | collective-permute-start | bytes 4325384 | tf_op jit(solution)/shard_map/ppermute | solution.py:17
  273.0 16.4 %collective-permute-start.38 = (bf16[288,1024]{1,0:T(8,128)(2,1)S(1)}, bf16[288,1024]{1,0:T(8,128)(2,1)S(1)}, u32[]{:S(2)}, u32[]{:S(2)}) collective-permute-start(bf16[288,1024]{1,0:T(8,128)(2,1)S(1)} %fusion.25), channel_id=1, source_target_pairs={{0,4},{2,6},{4,0},{6,2},{8,12},{10,14},{12,8},{14,10},{16,20},{18,... | collective-permute-start | bytes 1769480 | tf_op jit(solution)/shard_map/ppermute | solution.py:22
  276.8 16.3 %collective-permute-start.33 = (bf16[2,64,2304]{2,1,0:T(8,128)(2,1)S(1)}, bf16[2,64,2304]{2,1,0:T(8,128)(2,1)S(1)}, u32[]{:S(2)}, u32[]{:S(2)}) collective-permute-start(bf16[2,64,2304]{2,1,0:T(8,128)(2,1)S(1)} %fusion.27), channel_id=1, source_target_pairs={{0,2},{2,0},{4,6},{6,4},{8,10},{10,8},{12,14},{14,12},{16,18},{18,... | collective-permute-start | bytes 1769480 | tf_op jit(solution)/shard_map/ppermute | solution.py:22
  279.9 16.0 %collective-permute-start.28 = (bf16[2,64,2304]{2,1,0:T(8,128)(2,1)S(1)}, bf16[2,64,2304]{2,1,0:T(8,128)(2,1)S(1)}, u32[]{:S(2)}, u32[]{:S(2)}) collective-permute-start(bf16[2,64,2304]{2,1,0:T(8,128)(2,1)S(1)} %fusion.28), channel_id=1, source_target_pairs={{0,8},{2,10},{4,12},{6,14},{8,0},{10,2},{12,4},{14,6},{16,24},{18,... | collective-permute-start | bytes 1769480 | tf_op jit(solution)/shard_map/ppermute | solution.py:22
  280.1 26.5 %collective-permute-start.17 = (bf16[2,2,2,32,1408]{4,3,2,1,0:T(8,128)(2,1)S(1)}, bf16[2,2,2,32,1408]{4,3,2,1,0:T(8,128)(2,1)S(1)}, u32[]{:S(2)}, u32[]{:S(2)}) collective-permute-start(bf16[2,2,2,32,1408]{4,3,2,1,0:T(8,128)(2,1)S(1)} %fusion.22), channel_id=1, source_target_pairs={{0,2},{2,0},{4,6},{6,4},{8,10},{10,8},{12,14},{14,12},{16,18},{18,... | collective-permute-start | bytes 2162696 | tf_op jit(solution)/shard_map/ppermute | solution.py:22
  281.6 28.0 %collective-permute-start.22 = (bf16[2,2,2,32,1408]{4,3,2,1,0:T(8,128)(2,1)S(1)}, bf16[2,2,2,32,1408]{4,3,2,1,0:T(8,128)(2,1)S(1)}, u32[]{:S(2)}, u32[]{:S(2)}) collective-permute-start(bf16[2,2,2,32,1408]{4,3,2,1,0:T(8,128)(2,1)S(1)} %fusion.21), channel_id=1, source_target_pairs={{0,4},{2,6},{4,0},{6,2},{8,12},{10,14},{12,8},{14,10},{16,20},{18,... | collective-permute-start | bytes 2162696 | tf_op jit(solution)/shard_map/ppermute | solution.py:22
  289.3 31.6 %collective-permute-start.12 = (bf16[2,2,2,32,1408]{4,3,2,1,0:T(8,128)(2,1)S(1)}, bf16[2,2,2,32,1408]{4,3,2,1,0:T(8,128)(2,1)S(1)}, u32[]{:S(2)}, u32[]{:S(2)}) collective-permute-start(bf16[2,2,2,32,1408]{4,3,2,1,0:T(8,128)(2,1)S(1)} %fusion.23), channel_id=1, source_target_pairs={{0,8},{2,10},{4,12},{6,14},{8,0},{10,2},{12,4},{14,6},{16,24},{18,... | collective-permute-start | bytes 2162696 | tf_op jit(solution)/shard_map/ppermute | solution.py:22
  293.1 53.4 %collective-permute-start.39 = (bf16[288,1024]{1,0:T(8,128)(2,1)S(1)}, bf16[288,1024]{1,0:T(8,128)(2,1)S(1)}, u32[]{:S(2)}, u32[]{:S(2)}) collective-permute-start(bf16[288,1024]{1,0:T(8,128)(2,1)S(1)} %fusion.54), channel_id=1, source_target_pairs={{1,17},{3,19},{5,21},{7,23},{9,25},{11,27},{13,29},{15,31},{16,0},... | collective-permute-start | bytes 1769480 | tf_op jit(solution)/shard_map/ppermute | solution.py:191
  295.8 38.4 %collective-permute-start.34 = (bf16[64,2304]{1,0:T(8,128)(2,1)S(1)}, bf16[64,2304]{1,0:T(8,128)(2,1)S(1)}, u32[]{:S(2)}, u32[]{:S(2)}) collective-permute-start(bf16[64,2304]{1,0:T(8,128)(2,1)S(1)} %fusion.36), channel_id=1, source_target_pairs={{0,16},{2,18},{4,20},{6,22},{8,24},{10,26},{12,28},{14,30},{16,0},... | collective-permute-start | bytes 884744 | tf_op jit(solution)/shard_map/ppermute | solution.py:22
  306.7 30.7 %collective-permute-start.29 = (bf16[64,2304]{1,0:T(8,128)(2,1)S(1)}, bf16[64,2304]{1,0:T(8,128)(2,1)S(1)}, u32[]{:S(2)}, u32[]{:S(2)}) collective-permute-start(bf16[64,2304]{1,0:T(8,128)(2,1)S(1)} %fusion.38), channel_id=1, source_target_pairs={{0,16},{2,18},{4,20},{6,22},{8,24},{10,26},{12,28},{14,30},{16,0},... | collective-permute-start | bytes 884744 | tf_op jit(solution)/shard_map/ppermute | solution.py:22
  309.6 29.1 %collective-permute-start.18 = (bf16[2,2,32,1408]{3,2,1,0:T(8,128)(2,1)S(1)}, bf16[2,2,32,1408]{3,2,1,0:T(8,128)(2,1)S(1)}, u32[]{:S(2)}, u32[]{:S(2)}) collective-permute-start(bf16[2,2,32,1408]{3,2,1,0:T(8,128)(2,1)S(1)} %fusion.34), channel_id=1, source_target_pairs={{0,4},{2,6},{4,0},{6,2},{8,12},{10,14},{12,8},{14,10},{16,20},{18,... | collective-permute-start | bytes 1081352 | tf_op jit(solution)/shard_map/ppermute | solution.py:22
  321.0 18.4 %collective-permute-start.23 = (bf16[2,2,32,1408]{3,2,1,0:T(8,128)(2,1)S(1)}, bf16[2,2,32,1408]{3,2,1,0:T(8,128)(2,1)S(1)}, u32[]{:S(2)}, u32[]{:S(2)}) collective-permute-start(bf16[2,2,32,1408]{3,2,1,0:T(8,128)(2,1)S(1)} %fusion.33), channel_id=1, source_target_pairs={{0,8},{2,10},{4,12},{6,14},{8,0},{10,2},{12,4},{14,6},{16,24},{18,... | collective-permute-start | bytes 1081352 | tf_op jit(solution)/shard_map/ppermute | solution.py:22
  348.0 18.2 %collective-permute-start.40 = (f32[144,1024]{1,0:T(8,128)S(1)}, f32[144,1024]{1,0:T(8,128)S(1)}, u32[]{:S(2)}, u32[]{:S(2)}) collective-permute-start(f32[144,1024]{1,0:T(8,128)S(1)} %dynamic-slice_bitcast_fusion.5), channel_id=1, source_target_pairs={{0,1},{1,0},{2,3},{3,2},{4,5},{5,4},{6,7},{7,6},{8,9},{9,8},{10,11... | collective-permute-start | bytes 1769480 | tf_op jit(solution)/shard_map/ppermute | solution.py:17
  348.2 11.2 %collective-permute-start.20 = (bf16[32,1408]{1,0:T(8,128)(2,1)S(1)}, bf16[32,1408]{1,0:T(8,128)(2,1)S(1)}, u32[]{:S(2)}, u32[]{:S(2)}) collective-permute-start(bf16[32,1408]{1,0:T(8,128)(2,1)S(1)} %fusion.50), channel_id=1, source_target_pairs={{0,16},{2,18},{4,20},{6,22},{8,24},{10,26},{12,28},{14,30},{16,0},... | collective-permute-start | bytes 270344 | tf_op jit(solution)/shard_map/ppermute | solution.py:22
  348.4 13.0 %collective-permute-start.25 = (bf16[32,1408]{1,0:T(8,128)(2,1)S(1)}, bf16[32,1408]{1,0:T(8,128)(2,1)S(1)}, u32[]{:S(2)}, u32[]{:S(2)}) collective-permute-start(bf16[32,1408]{1,0:T(8,128)(2,1)S(1)} %fusion.48), channel_id=1, source_target_pairs={{0,16},{2,18},{4,20},{6,22},{8,24},{10,26},{12,28},{14,30},{16,0},... | collective-permute-start | bytes 270344 | tf_op jit(solution)/shard_map/ppermute | solution.py:22
  351.4 11.9 %collective-permute-start.15 = (bf16[32,1408]{1,0:T(8,128)(2,1)S(1)}, bf16[32,1408]{1,0:T(8,128)(2,1)S(1)}, u32[]{:S(2)}, u32[]{:S(2)}) collective-permute-start(bf16[32,1408]{1,0:T(8,128)(2,1)S(1)} %fusion.52), channel_id=1, source_target_pairs={{0,16},{2,18},{4,20},{6,22},{8,24},{10,26},{12,28},{14,30},{16,0},... | collective-permute-start | bytes 270344 | tf_op jit(solution)/shard_map/ppermute | solution.py:22
  (54 other events, 490.7 us)
